TPU v7x, 256 devices: a whole 4x4x8 slice. The times are simulated.
256 devices in a mesh: pair: 2 (over y_lo), narrow: 8 (over x, y_hi), wide: 16 (over z, core).
Axes of the slice: x: 4, y: 4 (y_hi: 2, y_lo: 2; y = y_hi * 2 + y_lo), z: 8, core: 2. Of those that a mesh axis runs over, the one named last changes fastest.
Arguments:
- frame_one: bfloat16 [98304, 128], P(('pair', 'narrow', 'wide')), parts along dimension 0, may hold values from -8 to 8
- frame_two: bfloat16 [98304, 128], P(('pair', 'wide', 'narrow')), parts along dimension 0, may hold values from -8 to 8
Outputs:
- flow_forward: float32 [2, 98304], P(None, ('pair', 'narrow', 'wide')), parts along dimension 1
- flow_backward: float32 [2, 98304], P(None, ('pair', 'wide', 'narrow')), parts along dimension 1
There are 2 independent parts, one for each index of `pair`. A program takes and returns all parts, laid end to end along the dimension named above; each array names one. Nothing has to cross between parts.
All inputs are finite; a program needn't handle non-finite values.
Results may differ from a plain program's by a relative error of at most 0.0003.
Values may be sent and summed in bfloat16 or wider, within the bound.
No kernel may reach another device: no remote copies, remote signals or barrier semaphores. Data moves between devices by JAX's collectives and lax.ppermute only.
A program may use at most 64 MiB of HBM per device.

v0:
```python
import functools
import math

import jax
import jax.numpy as jnp
from jax import lax
from jax.experimental import pallas as pl
from jax.experimental.pallas import tpu as pltpu
from jax.sharding import PartitionSpec as P

IMG_W = 384
LANES = 128
THIRDS = IMG_W // LANES
STRIPS = IMG_W // 8
LOWEST = -3.0e38
HIGH = 2.0**100
LOW = 2.0**-80
f32 = jnp.float32
bf16 = jnp.bfloat16
VMEM = pl.BlockSpec(memory_space=pltpu.VMEM)
SMEM = pl.BlockSpec(memory_space=pltpu.SMEM)


def matmul_nt(left, right):
    return lax.dot_general(left, right, (((1,), (1,)), ((), ())), preferred_element_type=f32)


def merged(first, second):
    peak = jnp.maximum(first[0:1], second[0:1])
    sums = first * jnp.exp2(first[0:1] - peak) + second * jnp.exp2(second[0:1] - peak)
    row = lax.broadcasted_iota(jnp.int32, first.shape, 0)
    return jnp.where(row == 0, peak, sums)


def match_kernel(n_rows, n_cols, n_pieces, scale, place, u_ref, *refs):
    pieces, refs = refs[:n_pieces], refs[n_pieces:]
    n_hops = n_cols // 4
    rows_ref, hop_refs, refs = refs[0], refs[1:1 + n_hops], refs[1 + n_hops:]
    (by_col_ref, u2, v2, score, part, flush, peaks, n_col, x_col, y_col, slow_row, slow_col, flags) = refs
    span = n_cols * LANES
    wide = THIRDS * span
    per_piece = n_cols // n_pieces

    for k in range(n_cols):
        piece, start = pieces[k // per_piece], k % per_piece * IMG_W
        to = pl.ds(pl.multiple_of(place[8 + k] * LANES, LANES), LANES)
        for g in range(THIRDS):
            v2[g, to, :] = piece[start + g * LANES:start + (g + 1) * LANES, :]

    def split(a, carry):
        at = pl.ds(pl.multiple_of(a * IMG_W, IMG_W), IMG_W)
        scaled = u_ref[at, :].astype(f32) * scale
        top = scaled.astype(bf16)
        u2[at, :LANES] = top
        u2[at, LANES:] = (scaled - top.astype(f32)).astype(bf16)
        return carry

    lax.fori_loop(0, n_rows, split, 0)

    def clear():
        nothing = jnp.zeros((8, wide), f32)
        n_col[...] = nothing
        x_col[...] = nothing
        y_col[...] = nothing
        slow_col[...] = jnp.where(lax.broadcasted_iota(jnp.int32, (4, wide), 0) == 0, LOWEST, 0.0)

    clear()

    def clear_row():
        slow_row[...] = jnp.where(lax.broadcasted_iota(jnp.int32, (IMG_W, LANES), 1) == 0, LOWEST, 0.0)

    def fast(a, slot, thirds):
        left = u2[pl.ds(pl.multiple_of(a * IMG_W, IMG_W), IMG_W), :]
        for g in thirds:
            right = v2[g]
            s = matmul_nt(left, jnp.concatenate([right, right], axis=1))
            n = x = None
            for h in range(STRIPS):
                at = slice(8 * h, 8 * h + 8)
                e = jnp.exp2(s[at, :])
                n = n + e if h else e
                x = x + n if h else e
                run = tot = e[:, :LANES]
                for k in range(LANES, span, LANES):
                    run = run + e[:, k:k + LANES]
                    tot = tot + run
                part[slot, g, at, :LANES] = run
                part[slot, g, at, LANES:] = tot
            flush[slot, g, 0] = n
            flush[slot, g, 1] = x
            top = n[:, :LANES]
            for k in range(LANES, span, LANES):
                top = jnp.maximum(top, n[:, k:k + LANES])
            peaks[slot, g] = top

    kind = lax.broadcasted_iota(jnp.int32, (4, 3 * LANES), 0)
    column = lax.broadcasted_iota(jnp.int32, (4, 3 * LANES), 1)
    first, second = column < LANES, column < 2 * LANES
    table = jnp.where(kind == 1, jnp.where(first, 1, 0), jnp.where(
        kind == 2, jnp.where(first, column, jnp.where(second, LANES, 0)), jnp.where(second, 0, kind // 3)))
    table = table.astype(bf16)
    table = jnp.concatenate([table, table], axis=1)

    def row_sums(slot):
        n = [part[slot, g, :, :LANES] for g in range(THIRDS)]
        y = [part[slot, g, :, LANES:] for g in range(THIRDS)]
        upper = n[1] + n[2]
        whole = jnp.concatenate([n[0] + upper, upper + n[2], y[0] + y[1] + y[2]], axis=1)
        top = whole.astype(bf16)
        rest = (whole - top.astype(f32)).astype(bf16)
        sums = matmul_nt(table, jnp.concatenate([top, rest], axis=1))
        row = lax.broadcasted_iota(jnp.int32, sums.shape, 0)
        return jnp.where(row == 3, (place[3] + n_cols).astype(f32) * sums[1:2] - sums, sums)

    def slow(a, g):
        left = u2[pl.ds(pl.multiple_of(a * IMG_W, IMG_W), IMG_W), :]
        offset = pl.multiple_of(g * span, span)

        right = v2[g]
        score[...] = matmul_nt(left, jnp.concatenate([right, right], axis=1))
        index = lax.broadcasted_iota(jnp.int32, (1, span), 1)
        down = (index // LANES + place[3]).astype(f32)
        across = (lax.rem(index, LANES) + g * LANES).astype(f32)
        column = lax.broadcasted_iota(jnp.int32, (8, LANES), 1)
        peak = None
        for h in range(STRIPS):
            at = slice(8 * h, 8 * h + 8)
            s = score[at, :]
            m = jnp.max(s, axis=1, keepdims=True)
            w = jnp.exp2(s - m)
            old = slow_row[at, :]
            new = jnp.where(column == 0, m, jnp.where(column == 1, jnp.sum(w, axis=1, keepdims=True), jnp.where(
                column == 2, jnp.sum(w * across, axis=1, keepdims=True), jnp.sum(w * down, axis=1, keepdims=True))))
            both = jnp.maximum(old[:, 0:1], m)
            sums = old * jnp.exp2(old[:, 0:1] - both) + new * jnp.exp2(m - both)
            slow_row[at, :] = jnp.where(column == 0, both, sums)
            peak = jnp.maximum(peak, s) if h else s
        peak = jnp.max(peak, axis=0, keepdims=True)
        n = x = None
        for h in range(STRIPS):
            w = jnp.exp2(score[8 * h:8 * h + 8, :] - peak)
            n = n + w if h else w
            x = x + n if h else w
        inner = lax.broadcasted_iota(jnp.int32, (8, 1), 0).astype(f32)
        x = 8.0 * (STRIPS * n - x) + n * inner
        n = jnp.sum(n, axis=0, keepdims=True)
        x = jnp.sum(x, axis=0, keepdims=True)
        row = lax.broadcasted_iota(jnp.int32, (4, span), 0)
        new = jnp.where(row == 0, peak, jnp.where(row == 1, n, jnp.where(row == 2, x, n * image_row(a))))
        at = pl.ds(offset, span)
        slow_col[:, at] = merged(slow_col[:, at], new)

    def image_row(a):
        return (place[0] + place[1] * a).astype(f32)

    def slow_stats():
        return jnp.transpose(slow_row[...])[0:4]

    def at_zero(stats):
        row = lax.broadcasted_iota(jnp.int32, stats.shape, 0)
        return jnp.where(row == 0, jnp.where(stats[1:2] > 0.0, 0.0, LOWEST), stats)

    def finish(a, slot, real):
        bad = [jnp.logical_not(jnp.max(peaks[slot, g]) < HIGH) for g in range(THIRDS)]
        for g in range(THIRDS):
            at = slice(g * span, (g + 1) * span)
            skip = jnp.logical_or(bad[g], jnp.logical_not(real))
            n = jnp.where(skip, 0.0, flush[slot, g, 0])
            x = jnp.where(skip, 0.0, flush[slot, g, 1])
            n_col[:, at] += n
            x_col[:, at] += x
            y_col[:, at] += n * image_row(a)
        rows_ref[a] = row_sums(slot)
        for g in range(THIRDS):
            flags[slot, g] = bad[g].astype(jnp.int32)
        return jnp.logical_and(real, jnp.logical_or(jnp.logical_or(bad[0], bad[1]), bad[2]))

    def repair(a, slot):
        clear_row()

        def third_of(g, carry):
            @pl.when(flags[slot, g] == 1)
            def _():
                part[slot, g] = jnp.zeros((IMG_W, 2 * LANES), f32)
                slow(a, g)
            return carry

        lax.fori_loop(0, THIRDS, third_of, 0)
        rows_ref[a] = merged(at_zero(row_sums(slot)), slow_stats())

    def two(i, carry):
        a = 2 * i
        slot = 2 * lax.rem(i, 2)
        before, was = jnp.maximum(a - 1, 0), 3 - slot
        again = finish(before, was, a > 0)
        fast(a, slot, range(THIRDS))
        fast(a + 1, slot + 1, range(1))
        again_too = finish(a, slot, a >= 0)
        fast(a + 1, slot + 1, range(1, THIRDS))

        @pl.when(jnp.logical_or(again, again_too))
        def _():
            def each(k, inner):
                @pl.when(jnp.where(k == 0, again, again_too))
                def _():
                    repair(jnp.where(k == 0, before, a), jnp.where(k == 0, was, slot))
                return inner

            lax.fori_loop(0, 2, each, 0)
        return carry

    lax.fori_loop(0, n_rows // 2, two, 0)
    last = n_rows - 1
    slot = 2 * ((n_rows // 2 - 1) % 2) + 1
    again = finish(last, slot, last >= 0)

    @pl.when(again)
    def _():
        repair(last, slot)

    def columns():
        n = n_col[...]
        inner = lax.broadcasted_iota(jnp.int32, n.shape, 0).astype(f32)
        x = 8.0 * (STRIPS * n - x_col[...]) + n * inner
        row = lax.broadcasted_iota(jnp.int32, (4, wide), 0)
        sums = [jnp.sum(k, axis=0, keepdims=True) for k in (n, x, y_col[...])]
        fast_sums = jnp.where(row == 1, sums[0], jnp.where(row == 2, sums[1], jnp.where(row == 3, sums[2], 0.0)))
        return merged(at_zero(fast_sums), slow_col[...])

    def put(stats):
        for b in range(n_cols):
            for g in range(THIRDS):
                by_col_ref[b, :, g * LANES:(g + 1) * LANES] = stats[:, g * span + b * LANES:g * span + (b + 1) * LANES]
        for k in range(n_cols):
            hop_refs[k // 4][k % 4 // 2, k % 2] = by_col_ref[place[8 + n_cols + k]]

    def least(stats):
        return jnp.min(stats[1:2] * jnp.exp2(stats[0:1]))

    stats = columns()
    put(stats)
    low = least(stats)
    rows_low = rows_ref[0][1:2] * jnp.exp2(rows_ref[0][0:1])
    for a in range(1, n_rows):
        rows_low = jnp.minimum(rows_low, rows_ref[a][1:2] * jnp.exp2(rows_ref[a][0:1]))
    low = jnp.minimum(low, jnp.min(rows_low))

    @pl.when(jnp.logical_not(low >= LOW))
    def _():
        clear()

        def whole_row(a, carry):
            clear_row()

            def one(g, inner):
                slow(a, g)
                return inner

            lax.fori_loop(0, THIRDS, one, 0)
            rows_ref[a] = slow_stats()
            return carry

        lax.fori_loop(0, n_rows, whole_row, 0)
        put(slow_col[...])


def match(place, u, pieces):
    n_rows, n_cols = u.shape[0] // IMG_W, sum(p.shape[0] for p in pieces) // IMG_W
    n_hops = n_cols // 4
    out = jax.ShapeDtypeStruct((2, 2, 4, IMG_W), f32)
    span = n_cols * LANES
    wide = THIRDS * span
    scale = math.log2(math.e) / math.sqrt(u.shape[1])
    return pl.pallas_call(
        functools.partial(match_kernel, n_rows, n_cols, len(pieces), scale),
        out_shape=(jax.ShapeDtypeStruct((n_rows, 4, IMG_W), f32),) + (out,) * n_hops,
        in_specs=[SMEM] + [VMEM] * (1 + len(pieces)),
        out_specs=(VMEM,) * (1 + n_hops),
        scratch_shapes=[
            pltpu.VMEM((n_cols, 4, IMG_W), f32),
            pltpu.VMEM((n_rows * IMG_W, 2 * LANES), bf16),
            pltpu.VMEM((THIRDS, span, LANES), bf16),
            pltpu.VMEM((IMG_W, span), f32),
            pltpu.VMEM((4, THIRDS, IMG_W, 2 * LANES), f32),
            pltpu.VMEM((4, THIRDS, 2, 8, span), f32),
            pltpu.VMEM((4, THIRDS, 8, LANES), f32),
            pltpu.VMEM((8, wide), f32),
            pltpu.VMEM((8, wide), f32),
            pltpu.VMEM((8, wide), f32),
            pltpu.VMEM((IMG_W, LANES), f32),
            pltpu.VMEM((4, wide), f32),
            pltpu.SMEM((4, THIRDS), jnp.int32),
        ],
        compiler_params=pltpu.CompilerParams(vmem_limit_bytes=56 * 1024 * 1024),
        name="match",
    )(place, u, *pieces)


def merged_parts(parts):
    peak = functools.reduce(jnp.maximum, [part[..., 0:1, :] for part in parts])
    sums = sum(part * jnp.exp2(part[..., 0:1, :] - peak) for part in parts)
    row = lax.broadcasted_iota(jnp.int32, sums.shape, sums.ndim - 2)
    return jnp.where(row == 0, peak, sums)


def flow_kernel(place, one, *refs):
    across = lax.broadcasted_iota(jnp.int32, (1, IMG_W), 1).astype(f32)
    first = one[0]
    for other in range(1, one.shape[0]):
        first = merged(first, one[other])
    mine, by_core, by_y, by_both, *outs = refs
    second = merged(merged(mine[...], by_core[...]), merged(by_y[0], by_both[1]))
    for k, (total, out) in enumerate(zip((first, second), outs)):
        down = place[4 + k].astype(f32)
        out[0:1, :] = (total[2:3] / total[1:2] - across) * (2.0 / (IMG_W - 1))
        out[1:2, :] = (total[3:4] / total[1:2] - down) * (2.0 / (place[6].astype(f32) - 1.0))


def flow(place, one, two):
    out = jax.ShapeDtypeStruct((2, IMG_W), f32)
    return pl.pallas_call(
        flow_kernel, out_shape=(out, out), in_specs=[SMEM] + [VMEM] * 5, out_specs=(VMEM, VMEM), name="flow"
    )(place, one, *two)


def on_device(frame_one, frame_two):
    n_wide, n_narrow = lax.axis_size("wide"), lax.axis_size("narrow")
    n_z, n_x = n_wide // 2, n_narrow // 2
    w, n = lax.axis_index("wide"), lax.axis_index("narrow")
    z, core = w >> 1, w & 1
    x, y = n >> 1, n & 1
    along_z = [[2 * k for k in range(n_z)], [2 * k + 1 for k in reversed(range(n_z))]]
    flip = [(k, k ^ 1) for k in range(n_wide)]
    flip_y = [(k, k ^ 1) for k in range(n_narrow)]
    hops = [0, 1, n_x - 1] + list(range(2, n_x - 1))

    def along_x(array, hop):
        return lax.ppermute(array, "narrow", [(k, (k + 2 * hop) % n_narrow) for k in range(n_narrow)])

    u = lax.all_to_all(jnp.broadcast_to(frame_one, (n_z,) + frame_one.shape), "wide", 0, 0, axis_index_groups=along_z)
    both = jnp.concatenate([frame_two, lax.ppermute(frame_two, "narrow", flip_y)])
    pieces = [both] + [along_x(both, hop) for hop in hops[1:]]
    pieces += [lax.ppermute(piece, "wide", flip) for piece in pieces]
    goes = [(core ^ c) * n_narrow + lax.rem(x + (n_x - hop), n_x) * 2 + (y ^ k) for c in range(2) for hop in hops for k in range(2)]
    sends = [(core ^ c) * n_narrow + lax.rem(x + hop, n_x) * 2 + (y ^ k) for hop in range(n_x) for c in range(2) for k in range(2)]
    own = [n * n_wide + w, w * n_narrow + n, n_wide * n_narrow, 0]
    place = jnp.stack([jnp.asarray(k, jnp.int32) for k in [n * n_wide + core + core * 2 * (n_z - 1), 2 - 4 * core, core, 2 * z * n_narrow] + own + goes + sends])
    rows, *parts = match(place, u.reshape(-1, frame_one.shape[1]), pieces)
    rows = lax.all_to_all(rows, "wide", 0, 0, axis_index_groups=along_z)
    parts = [parts[0]] + [along_x(parts[hop], hop) for hop in hops[1:]]
    by_y = lax.ppermute(merged_parts([part[:, 1] for part in parts]), "narrow", flip_y)
    mine = merged_parts([part[0, 0] for part in parts])
    by_core = lax.ppermute(merged_parts([part[1, 0] for part in parts]), "wide", flip)
    by_both = lax.ppermute(by_y, "wide", flip)
    return flow(place, rows, [mine, by_core, by_y, by_both])


def solution(mesh):
    placed = (P(("pair", "narrow", "wide"), None), P(("pair", "wide", "narrow"), None))
    return jax.shard_map(
        on_device,
        mesh=mesh,
        in_specs=placed,
        out_specs=(P(None, ("pair", "narrow", "wide")), P(None, ("pair", "wide", "narrow"))),
        check_vma=False,
    )
```

profile of v0, /device:TPU:8, one launch (start us, length us, event | category | flops | bytes accessed | tf_op | source)
XLA Modules:
  0.0 87.0 jit_solution(9850166510615515531)
XLA Ops:
  0.6 1.9 %broadcast_in_dim.26 = bf16[8,384,128]{2,1,0:T(8,128)(2,1)} broadcast(bf16[384,128]{1,0:T(8,128)(2,1)} %param.2), dimensions={1,2} | broadcast | bytes 884736 | tf_op jit(solution)/shard_map/broadcast_in_dim | solution.py:340
  2.5 8.6 %all-to-all-start = ((bf16[8,384,128]{2,1,0:T(8,128)(2,1)}), bf16[8,384,128]{2,1,0:T(8,128)(2,1)S(1)}, u32[]{:S(2)}, u32[]{:S(2)}) async-start(bf16[8,384,128]{2,1,0:T(8,128)(2,1)} %broadcast_in_dim.26), calls=%async_computation | async-start | bytes 1572864 | tf_op jit(solution)/shard_map/all_to_all | solution.py:340
  11.1 0.0 copy-done.10
  11.1 2.4 %collective-permute-start = (bf16[384,128]{1,0:T(8,128)(2,1)S(1)}, bf16[384,128]{1,0:T(8,128)(2,1)S(1)}, u32[]{:S(2)}, u32[]{:S(2)}) collective-permute-start(bf16[384,128]{1,0:T(8,128)(2,1)S(1)} %copy-done.10), channel_id=1, source_target_pairs={{0,16},{16,0},{32,48},{48,32},{64,80},{80,64},{96,112},{112,96},{1... | collective-permute-start | bytes 294920 | tf_op jit(solution)/shard_map/ppermute | solution.py:341
  13.5 4.2 %collective-permute-done = bf16[384,128]{1,0:T(8,128)(2,1)S(1)} collective-permute-done((bf16[384,128]{1,0:T(8,128)(2,1)S(1)}, bf16[384,128]{1,0:T(8,128)(2,1)S(1)}, u32[]{:S(2)}, u32[]{:S(2)}) %collective-permute-start) | collective-permute-done | bytes 98336 | tf_op jit(solution)/shard_map/ppermute | solution.py:341
  17.8 1.6 %collective-permute-start.1 = (bf16[768,128]{1,0:T(8,128)(2,1)S(1)}, bf16[768,128]{1,0:T(8,128)(2,1)S(1)}, u32[]{:S(2)}, u32[]{:S(2)}) collective-permute-start(bf16[768,128]{1,0:T(8,128)(2,1)S(1)} %constant_dynamic-update-slice_fusion.refs_0_), channel_id=1, source_target_pairs={{0,32},{16,48},{32,64},{48,80},{64,96},{80,112},{96,0},{112,16},{1... | collective-permute-start | bytes 589832 | tf_op jit(solution)/shard_map/ppermute | solution.py:338
  19.3 1.7 %collective-permute-start.2 = (bf16[768,128]{1,0:T(8,128)(2,1)S(1)}, bf16[768,128]{1,0:T(8,128)(2,1)S(1)}, u32[]{:S(2)}, u32[]{:S(2)}) collective-permute-start(bf16[768,128]{1,0:T(8,128)(2,1)S(1)} %constant_dynamic-update-slice_fusion.refs_0_), channel_id=1, source_target_pairs={{0,96},{16,112},{32,0},{48,16},{64,32},{80,48},{96,64},{112,80},{1... | collective-permute-start | bytes 589832 | tf_op jit(solution)/shard_map/ppermute | solution.py:338
  21.1 1.8 %collective-permute-start.3 = (bf16[768,128]{1,0:T(8,128)(2,1)S(1)}, bf16[768,128]{1,0:T(8,128)(2,1)S(1)}, u32[]{:S(2)}, u32[]{:S(2)}) collective-permute-start(bf16[768,128]{1,0:T(8,128)(2,1)S(1)} %constant_dynamic-update-slice_fusion.refs_0_), channel_id=1, source_target_pairs={{0,64},{16,80},{32,96},{48,112},{64,0},{80,16},{96,32},{112,48},{1... | collective-permute-start | bytes 589832 | tf_op jit(solution)/shard_map/ppermute | solution.py:338
  22.9 0.0 collective-permute-start.4
  22.9 3.0 %collective-permute-done.1.refs_1_ = bf16[768,128]{1,0:T(8,128)(2,1)S(1)} collective-permute-done((bf16[768,128]{1,0:T(8,128)(2,1)S(1)}, bf16[768,128]{1,0:T(8,128)(2,1)S(1)}, u32[]{:S(2)}, u32[]{:S(2)}) %collective-permute-start.1) | collective-permute-done | bytes 196640 | tf_op jit(solution)/shard_map/ppermute | solution.py:338
  25.9 0.0 collective-permute-start.5
  25.9 3.0 %collective-permute-done.2.refs_2_ = bf16[768,128]{1,0:T(8,128)(2,1)S(1)} collective-permute-done((bf16[768,128]{1,0:T(8,128)(2,1)S(1)}, bf16[768,128]{1,0:T(8,128)(2,1)S(1)}, u32[]{:S(2)}, u32[]{:S(2)}) %collective-permute-start.2) | collective-permute-done | bytes 196640 | tf_op jit(solution)/shard_map/ppermute | solution.py:338
  28.9 0.0 collective-permute-start.6
  28.9 1.7 %collective-permute-done.3.refs_3_ = bf16[768,128]{1,0:T(8,128)(2,1)S(1)} collective-permute-done((bf16[768,128]{1,0:T(8,128)(2,1)S(1)}, bf16[768,128]{1,0:T(8,128)(2,1)S(1)}, u32[]{:S(2)}, u32[]{:S(2)}) %collective-permute-start.3) | collective-permute-done | bytes 196640 | tf_op jit(solution)/shard_map/ppermute | solution.py:338
  30.6 0.0 collective-permute-start.7
  30.6 0.6 stack.119.place
  31.3 0.0 collective-permute-done.4.refs_4_
  31.3 0.0 collective-permute-done.5.refs_5_
  31.3 0.0 collective-permute-done.6.refs_6_
  31.3 0.8 collective-permute-done.7.refs_7_
  32.1 0.0 all-to-all-done
  32.1 0.0 copy-done.1
  32.1 0.6 copy-done.8
  32.7 0.3 copy-done
  33.0 27.9 %match.1 = (f32[8,4,384]{2,1,0:T(4,128)}, f32[2,2,4,384]{3,2,1,0:T(4,128)}, f32[2,2,4,384]{3,2,1,0:T(4,128)}, f32[2,2,4,384]{3,2,1,0:T(4,128)}, f32[2,2,4,384]{3,2,1,0:T(4,128)}) custom-call(s32[40]{0:T(128)} %stack.119.place, bf16[3072,128]{1,0:T(8,128)(2,1)} %bitcast.112, bf16[768,128]{1,0:T(8,128)(2,1)} %copy-done.1, bf16[768,128]{1,0:T(8,128)(2,1)} %copy-done.2, ...), custom_call_target="tpu_custom_call" | custom-call | tf_op jit(solution)/shard_map/match/pallas_call | solution.py:274
  61.0 0.1 collective-permute-start.10
  61.0 0.7 slice_bitcast_fusion.3
  61.8 10.4 %all-to-all-start.1 = ((f32[8,4,384]{2,1,0:T(4,128)}), f32[8,4,384]{2,1,0:T(4,128)S(1)}, u32[]{:S(2)}, u32[]{:S(2)}) async-start(f32[8,4,384]{2,1,0:T(4,128)} %get-tuple-element.7), calls=%async_computation.1 | async-start | bytes 98304 | tf_op jit(solution)/shard_map/all_to_all | solution.py:349
  72.2 0.1 collective-permute-start.9
  72.3 0.0 copy-done.12
  72.3 2.0 %collective-permute-start.8 = (f32[2,2,4,384]{3,2,0,1:T(4,128)S(1)}, f32[2,2,4,384]{3,2,0,1:T(4,128)S(1)}, u32[]{:S(2)}, u32[]{:S(2)}) collective-permute-start(f32[2,2,4,384]{3,2,0,1:T(4,128)S(1)} %copy.4), channel_id=1, source_target_pairs={{0,32},{16,48},{32,64},{48,80},{64,96},{80,112},{96,0},{112,16},{1... | collective-permute-start | bytes 73736 | tf_op jit(solution)/shard_map/ppermute | solution.py:338
  74.3 0.0 collective-permute-done.10
  74.3 1.8 %collective-permute-done.9 = f32[2,2,4,384]{3,2,1,0:T(4,128)S(1)} collective-permute-done((f32[2,2,4,384]{3,2,1,0:T(4,128)S(1)}, f32[2,2,4,384]{3,2,1,0:T(4,128)S(1)}, u32[]{:S(2)}, u32[]{:S(2)}) %collective-permute-start.9) | collective-permute-done | bytes 24608 | tf_op jit(solution)/shard_map/ppermute | solution.py:338
  76.1 1.3 %collective-permute-done.8 = f32[2,2,4,384]{3,2,0,1:T(4,128)S(1)} collective-permute-done((f32[2,2,4,384]{3,2,0,1:T(4,128)S(1)}, f32[2,2,4,384]{3,2,0,1:T(4,128)S(1)}, u32[]{:S(2)}, u32[]{:S(2)}) %collective-permute-start.8) | collective-permute-done | bytes 24608 | tf_op jit(solution)/shard_map/ppermute | solution.py:338
  77.5 0.1 add_select_fusion
  77.6 0.0 collective-permute-start.12
  77.8 5.1 %collective-permute-done.12.refs_2_ = f32[2,4,384]{2,1,0:T(4,128)S(1)} collective-permute-done((f32[2,4,384]{2,1,0:T(4,128)S(1)}, f32[2,4,384]{2,1,0:T(4,128)S(1)}, u32[]{:S(2)}, u32[]{:S(2)}) %collective-permute-start.12) | collective-permute-done | bytes 12320 | tf_op jit(solution)/shard_map/ppermute | solution.py:351
  82.8 0.0 collective-permute-start.13
  82.8 0.7 fusion.2
  83.5 0.5 collective-permute-start.11
  84.0 0.8 collective-permute-done.11.refs_1_
  84.8 0.0 collective-permute-done.13.refs_3_
  84.8 0.0 all-to-all-done.1.one
  84.8 0.0 copy-start.9
  84.8 0.6 copy-done.15
  85.4 0.0 copy-done.14
  85.4 0.0 copy-done.9
  85.5 1.6 %flow.1 = (f32[2,384]{1,0:T(2,128)}, f32[2,384]{1,0:T(2,128)}) custom-call(s32[40]{0:T(128)} %stack.119.place, f32[8,4,384]{2,1,0:T(4,128)} %copy-done.9, f32[4,384]{1,0:T(4,128)} %get-tuple-element.27.refs_0_, f32[4,384]{1,0:T(4,128)} %copy-done.15, f32[2,4,384]{2,1,0:T(4,128)} %copy-done.13, f32[2,4,384]{2,1,0:T(4,128)} %copy-done.14), custom_call_target="tpu_custom_call" | custom-call | tf_op jit(solution)/shard_map/flow/pallas_call | solution.py:321
  (44 shorter events, 0.3 us)
Async XLA Ops:
  2.5 8.6 %copy-start.10 = (bf16[384,128]{1,0:T(8,128)(2,1)S(1)}, bf16[384,128]{1,0:T(8,128)(2,1)}, u32[]{:S(2)}) copy-start(bf16[384,128]{1,0:T(8,128)(2,1)} %param.3) | copy-start | bytes 294916
  2.5 29.6 %all-to-all-start = ((bf16[8,384,128]{2,1,0:T(8,128)(2,1)}), bf16[8,384,128]{2,1,0:T(8,128)(2,1)S(1)}, u32[]{:S(2)}, u32[]{:S(2)}) async-start(bf16[8,384,128]{2,1,0:T(8,128)(2,1)} %broadcast_in_dim.26), calls=%async_computation | async-start | bytes 1572864 | tf_op jit(solution)/shard_map/all_to_all | solution.py:340
  11.1 6.6 %collective-permute-start = (bf16[384,128]{1,0:T(8,128)(2,1)S(1)}, bf16[384,128]{1,0:T(8,128)(2,1)S(1)}, u32[]{:S(2)}, u32[]{:S(2)}) collective-permute-start(bf16[384,128]{1,0:T(8,128)(2,1)S(1)} %copy-done.10), channel_id=1, source_target_pairs={{0,16},{16,0},{32,48},{48,32},{64,80},{80,64},{96,112},{112,96},{1... | collective-permute-start | bytes 294920 | tf_op jit(solution)/shard_map/ppermute | solution.py:341
  17.8 14.3 %copy-start.1 = (bf16[768,128]{1,0:T(8,128)(2,1)}, bf16[768,128]{1,0:T(8,128)(2,1)S(1)}, u32[]{:S(2)}) copy-start(bf16[768,128]{1,0:T(8,128)(2,1)S(1)} %constant_dynamic-update-slice_fusion.refs_0_) | copy-start | bytes 589828
  17.8 8.1 %collective-permute-start.1 = (bf16[768,128]{1,0:T(8,128)(2,1)S(1)}, bf16[768,128]{1,0:T(8,128)(2,1)S(1)}, u32[]{:S(2)}, u32[]{:S(2)}) collective-permute-start(bf16[768,128]{1,0:T(8,128)(2,1)S(1)} %constant_dynamic-update-slice_fusion.refs_0_), channel_id=1, source_target_pairs={{0,32},{16,48},{32,64},{48,80},{64,96},{80,112},{96,0},{112,16},{1... | collective-permute-start | bytes 589832 | tf_op jit(solution)/shard_map/ppermute | solution.py:338
  19.3 9.6 %collective-permute-start.2 = (bf16[768,128]{1,0:T(8,128)(2,1)S(1)}, bf16[768,128]{1,0:T(8,128)(2,1)S(1)}, u32[]{:S(2)}, u32[]{:S(2)}) collective-permute-start(bf16[768,128]{1,0:T(8,128)(2,1)S(1)} %constant_dynamic-update-slice_fusion.refs_0_), channel_id=1, source_target_pairs={{0,96},{16,112},{32,0},{48,16},{64,32},{80,48},{96,64},{112,80},{1... | collective-permute-start | bytes 589832 | tf_op jit(solution)/shard_map/ppermute | solution.py:338
  21.1 9.5 %collective-permute-start.3 = (bf16[768,128]{1,0:T(8,128)(2,1)S(1)}, bf16[768,128]{1,0:T(8,128)(2,1)S(1)}, u32[]{:S(2)}, u32[]{:S(2)}) collective-permute-start(bf16[768,128]{1,0:T(8,128)(2,1)S(1)} %constant_dynamic-update-slice_fusion.refs_0_), channel_id=1, source_target_pairs={{0,64},{16,80},{32,96},{48,112},{64,0},{80,16},{96,32},{112,48},{1... | collective-permute-start | bytes 589832 | tf_op jit(solution)/shard_map/ppermute | solution.py:338
  22.9 8.4 %collective-permute-start.4 = (bf16[768,128]{1,0:T(8,128)(2,1)S(1)}, bf16[768,128]{1,0:T(8,128)(2,1)S(1)}, u32[]{:S(2)}, u32[]{:S(2)}) collective-permute-start(bf16[768,128]{1,0:T(8,128)(2,1)S(1)} %constant_dynamic-update-slice_fusion.refs_0_), channel_id=1, source_target_pairs={{0,1},{1,0},{2,3},{3,2},{4,5},{5,4},{6,7},{7,6},{8,9},{9,8},{10,11... | collective-permute-start | bytes 589832 | tf_op jit(solution)/shard_map/ppermute | solution.py:343
  25.9 6.2 %copy-start.2 = (bf16[768,128]{1,0:T(8,128)(2,1)}, bf16[768,128]{1,0:T(8,128)(2,1)S(1)}, u32[]{:S(2)}) copy-start(bf16[768,128]{1,0:T(8,128)(2,1)S(1)} %collective-permute-done.1.refs_1_) | copy-start | bytes 589828
  25.9 5.4 %collective-permute-start.5 = (bf16[768,128]{1,0:T(8,128)(2,1)S(1)}, bf16[768,128]{1,0:T(8,128)(2,1)S(1)}, u32[]{:S(2)}, u32[]{:S(2)}) collective-permute-start(bf16[768,128]{1,0:T(8,128)(2,1)S(1)} %collective-permute-done.1.refs_1_), channel_id=1, source_target_pairs={{0,1},{1,0},{2,3},{3,2},{4,5},{5,4},{6,7},{7,6},{8,9},{9,8},{10,11... | collective-permute-start | bytes 589832 | tf_op jit(solution)/shard_map/ppermute | solution.py:343
  28.9 3.2 %copy-start.3 = (bf16[768,128]{1,0:T(8,128)(2,1)}, bf16[768,128]{1,0:T(8,128)(2,1)S(1)}, u32[]{:S(2)}) copy-start(bf16[768,128]{1,0:T(8,128)(2,1)S(1)} %collective-permute-done.2.refs_2_) | copy-start | bytes 589828
  28.9 2.4 %collective-permute-start.6 = (bf16[768,128]{1,0:T(8,128)(2,1)S(1)}, bf16[768,128]{1,0:T(8,128)(2,1)S(1)}, u32[]{:S(2)}, u32[]{:S(2)}) collective-permute-start(bf16[768,128]{1,0:T(8,128)(2,1)S(1)} %collective-permute-done.2.refs_2_), channel_id=1, source_target_pairs={{0,1},{1,0},{2,3},{3,2},{4,5},{5,4},{6,7},{7,6},{8,9},{9,8},{10,11... | collective-permute-start | bytes 589832 | tf_op jit(solution)/shard_map/ppermute | solution.py:343
  30.6 1.5 %copy-start.4 = (bf16[768,128]{1,0:T(8,128)(2,1)}, bf16[768,128]{1,0:T(8,128)(2,1)S(1)}, u32[]{:S(2)}) copy-start(bf16[768,128]{1,0:T(8,128)(2,1)S(1)} %collective-permute-done.3.refs_3_) | copy-start | bytes 589828
  30.6 1.4 %collective-permute-start.7 = (bf16[768,128]{1,0:T(8,128)(2,1)S(1)}, bf16[768,128]{1,0:T(8,128)(2,1)S(1)}, u32[]{:S(2)}, u32[]{:S(2)}) collective-permute-start(bf16[768,128]{1,0:T(8,128)(2,1)S(1)} %collective-permute-done.3.refs_3_), channel_id=1, source_target_pairs={{0,1},{1,0},{2,3},{3,2},{4,5},{5,4},{6,7},{7,6},{8,9},{9,8},{10,11... | collective-permute-start | bytes 589832 | tf_op jit(solution)/shard_map/ppermute | solution.py:343
  31.3 0.8 copy-start.5
  31.3 0.8 copy-start.6
  31.3 0.8 copy-start.7
  32.1 0.7 copy-start.8
  32.1 1.0 %copy-start = (bf16[8,384,128]{2,1,0:T(8,128)(2,1)}, bf16[8,384,128]{2,1,0:T(8,128)(2,1)S(1)}, u32[]{:S(2)}) copy-start(bf16[8,384,128]{2,1,0:T(8,128)(2,1)S(1)} %all-to-all-done) | copy-start | bytes 2359300
  60.9 0.8 copy-start.11
  61.0 13.3 %collective-permute-start.10 = (f32[2,2,4,384]{3,2,1,0:T(4,128)}, f32[2,2,4,384]{3,2,1,0:T(4,128)S(1)}, u32[]{:S(2)}, u32[]{:S(2)}) collective-permute-start(f32[2,2,4,384]{3,2,1,0:T(4,128)} %get-tuple-element.11), channel_id=1, source_target_pairs={{0,64},{16,80},{32,96},{48,112},{64,0},{80,16},{96,32},{112,48},{1... | collective-permute-start | bytes 73736 | tf_op jit(solution)/shard_map/ppermute | solution.py:338
  61.8 10.4 %copy-start.16 = (f32[2,2,4,384]{3,2,1,0:T(4,128)S(1)}, f32[2,2,4,384]{3,2,1,0:T(4,128)}, u32[]{:S(2)}) copy-start(f32[2,2,4,384]{3,2,1,0:T(4,128)} %get-tuple-element.10) | copy-start | bytes 73732
  61.8 10.5 %copy-start.12 = (f32[2,2,4,384]{3,2,1,0:T(4,128)S(1)}, f32[2,2,4,384]{3,2,1,0:T(4,128)}, u32[]{:S(2)}) copy-start(f32[2,2,4,384]{3,2,1,0:T(4,128)} %get-tuple-element.9) | copy-start | bytes 73732
  61.8 23.0 %all-to-all-start.1 = ((f32[8,4,384]{2,1,0:T(4,128)}), f32[8,4,384]{2,1,0:T(4,128)S(1)}, u32[]{:S(2)}, u32[]{:S(2)}) async-start(f32[8,4,384]{2,1,0:T(4,128)} %get-tuple-element.7), calls=%async_computation.1 | async-start | bytes 98304 | tf_op jit(solution)/shard_map/all_to_all | solution.py:349
  72.2 3.9 %collective-permute-start.9 = (f32[2,2,4,384]{3,2,1,0:T(4,128)S(1)}, f32[2,2,4,384]{3,2,1,0:T(4,128)S(1)}, u32[]{:S(2)}, u32[]{:S(2)}) collective-permute-start(f32[2,2,4,384]{3,2,1,0:T(4,128)S(1)} %copy-done.16), channel_id=1, source_target_pairs={{0,96},{16,112},{32,0},{48,16},{64,32},{80,48},{96,64},{112,80},{1... | collective-permute-start | bytes 73736 | tf_op jit(solution)/shard_map/ppermute | solution.py:338
  72.3 5.1 %collective-permute-start.8 = (f32[2,2,4,384]{3,2,0,1:T(4,128)S(1)}, f32[2,2,4,384]{3,2,0,1:T(4,128)S(1)}, u32[]{:S(2)}, u32[]{:S(2)}) collective-permute-start(f32[2,2,4,384]{3,2,0,1:T(4,128)S(1)} %copy.4), channel_id=1, source_target_pairs={{0,32},{16,48},{32,64},{48,80},{64,96},{80,112},{96,0},{112,16},{1... | collective-permute-start | bytes 73736 | tf_op jit(solution)/shard_map/ppermute | solution.py:338
  77.6 5.2 %collective-permute-start.12 = (f32[2,4,384]{2,1,0:T(4,128)S(1)}, f32[2,4,384]{2,1,0:T(4,128)S(1)}, u32[]{:S(2)}, u32[]{:S(2)}) collective-permute-start(f32[2,4,384]{2,1,0:T(4,128)S(1)} %add_select_fusion), channel_id=1, source_target_pairs={{0,16},{16,0},{32,48},{48,32},{64,80},{80,64},{96,112},{112,96},{1... | collective-permute-start | bytes 36872 | tf_op jit(solution)/shard_map/ppermute | solution.py:351
  82.8 0.7 copy-start.13
  82.8 2.0 %collective-permute-start.13 = (f32[2,4,384]{2,1,0:T(4,128)S(1)}, f32[2,4,384]{2,1,0:T(4,128)S(1)}, u32[]{:S(2)}, u32[]{:S(2)}) collective-permute-start(f32[2,4,384]{2,1,0:T(4,128)S(1)} %collective-permute-done.12.refs_2_), channel_id=1, source_target_pairs={{0,1},{1,0},{2,3},{3,2},{4,5},{5,4},{6,7},{7,6},{8,9},{9,8},{10,11... | collective-permute-start | bytes 36872 | tf_op jit(solution)/shard_map/ppermute | solution.py:354
  83.5 1.3 %collective-permute-start.11 = (f32[4,384]{1,0:T(4,128)S(1)}, f32[4,384]{1,0:T(4,128)S(1)}, u32[]{:S(2)}, u32[]{:S(2)}) collective-permute-start(f32[4,384]{1,0:T(4,128)S(1)} %get-tuple-element.26), channel_id=1, source_target_pairs={{0,1},{1,0},{2,3},{3,2},{4,5},{5,4},{6,7},{7,6},{8,9},{9,8},{10,11... | collective-permute-start | bytes 18440 | tf_op jit(solution)/shard_map/ppermute | solution.py:353
  84.8 0.6 copy-start.15
  84.8 0.6 copy-start.14
  84.8 0.6 copy-start.9
where the time goes:
time: 87 us
  Pallas kernels  29.5 us (34%)
  starting transfers between devices  29.2 us (34%)
  waiting for transfers between devices  21.7 us (25%)
  local copies, waits for them, and re-layouts  4.9 us (6%)
  between operations  0.88 us (1%)
    pallas_call x1, Pallas kernels, match(): pl.pallas_call(functools.partial(match_kernel, n_rows, n_cols, len(pieces...  27.9 us
    ppermute x6, waiting for transfers between devices, along_x(): lax.ppermute(array, 'narrow', [(k, (k + 2 * hop) % n_narrow) for k in ran...  10.8 us
    all_to_all x1, starting transfers between devices, on_device(): rows = lax.all_to_all(rows, 'wide', 0, 0, axis_index_groups=along_z)  10.4 us
    all_to_all x1, starting transfers between devices, on_device(): lax.all_to_all(jnp.broadcast_to(frame_one, (n_z,) + frame_one.shape), 'wi...  8.6 us
    ppermute x6, starting transfers between devices, along_x(): lax.ppermute(array, 'narrow', [(k, (k + 2 * hop) % n_narrow) for k in ran...  7.29 us
    ppermute x1, waiting for transfers between devices, on_device(): lax.ppermute(merged_parts([part[:, 1] for part in parts]), 'narrow', flip_y)  5.06 us
    ppermute x1, waiting for transfers between devices, on_device(): lax.ppermute(frame_two, 'narrow', flip_y)  4.25 us
    ppermute x1, starting transfers between devices, on_device(): lax.ppermute(frame_two, 'narrow', flip_y)  2.38 us
  transfers between devices with their start and end apart: 16, of which 9 were waited for; matrix products, arithmetic and copies ran while one was open for 3% of the time, Pallas kernels for 0%

commit v1 on v0

--- a/solution.py
+++ b/solution.py
@@ -351,6 +351,7 @@
     by_y = lax.ppermute(merged_parts([part[:, 1] for part in parts]), "narrow", flip_y)
     mine = merged_parts([part[0, 0] for part in parts])
     by_core = lax.ppermute(merged_parts([part[1, 0] for part in parts]), "wide", flip)
+    rows, mine, by_core, by_y = lax.optimization_barrier((rows, mine, by_core, by_y))
     by_both = lax.ppermute(by_y, "wide", flip)
     return flow(place, rows, [mine, by_core, by_y, by_both])
 

time: 87 us -> 86.5 us (level)
  starting transfers between devices: 29.2 us -> 27.6 us
    all_to_all x1, starting transfers between devices: 10.4 us -> 7.54 us  [on_device(): rows = lax.all_to_all(rows, 'wide', 0, 0, axis_index_groups=along_z)]
    ppermute x1, waiting for transfers between devices: 5.06 us -> 3.22 us  [on_device(): lax.ppermute(merged_parts([part[:, 1] for part in parts]), 'narrow', flip_y)]
    ppermute x6, starting transfers between devices: 7.29 us -> 8.93 us  [along_x(): lax.ppermute(array, 'narrow', [(k, (k + 2 * hop) % n_narrow) for k in ran...]
    ppermute x1, waiting for transfers between devices: 0.01 us -> 1.16 us  [on_device(): by_both = lax.ppermute(by_y, 'wide', flip)]
    ppermute x6, waiting for transfers between devices: 10.8 us -> 11.8 us  [along_x(): lax.ppermute(array, 'narrow', [(k, (k + 2 * hop) % n_narrow) for k in ran...]
  transfers between devices with their start and end apart: 16 -> 16, of which waited for: 9 -> 10; matrix products, arithmetic and copies ran while one was open for 3% -> 3% of each run, Pallas kernels for 0% -> 0%
where the time goes in v1:
time: 86.5 us; the launch traced here: 86 us
  Pallas kernels  29.5 us (34%)
  starting transfers between devices  27.6 us (32%)
  waiting for transfers between devices  22.3 us (26%)
  local copies, waits for them, and re-layouts  4.87 us (6%)
  between operations  0.87 us (1%)
    pallas_call x1, Pallas kernels, match(): pl.pallas_call(functools.partial(match_kernel, n_rows, n_cols, len(pieces...  27.9 us
    ppermute x6, waiting for transfers between devices, along_x(): lax.ppermute(array, 'narrow', [(k, (k + 2 * hop) % n_narrow) for k in ran...  11.8 us
    ppermute x6, starting transfers between devices, along_x(): lax.ppermute(array, 'narrow', [(k, (k + 2 * hop) % n_narrow) for k in ran...  8.93 us
    all_to_all x1, starting transfers between devices, on_device(): lax.all_to_all(jnp.broadcast_to(frame_one, (n_z,) + frame_one.shape), 'wi...  8.6 us
    all_to_all x1, starting transfers between devices, on_device(): rows = lax.all_to_all(rows, 'wide', 0, 0, axis_index_groups=along_z)  7.54 us
    ppermute x1, waiting for transfers between devices, on_device(): lax.ppermute(frame_two, 'narrow', flip_y)  4.25 us
    ppermute x1, waiting for transfers between devices, on_device(): lax.ppermute(merged_parts([part[:, 1] for part in parts]), 'narrow', flip_y)  3.22 us
    ppermute x1, starting transfers between devices, on_device(): lax.ppermute(frame_two, 'narrow', flip_y)  2.38 us
  transfers between devices with their start and end apart: 16, of which 10 were waited for; matrix products, arithmetic and copies ran while one was open for 3% of the time, Pallas kernels for 0%

profile of v1, /device:TPU:8, one launch (start us, length us, event | category | flops | bytes accessed | tf_op | source)
XLA Modules:
  0.0 86.0 jit_solution(471262169673538221)
XLA Ops:
  0.6 1.9 %broadcast_in_dim.26 = bf16[8,384,128]{2,1,0:T(8,128)(2,1)} broadcast(bf16[384,128]{1,0:T(8,128)(2,1)} %param.2), dimensions={1,2} | broadcast | bytes 884736 | tf_op jit(solution)/shard_map/broadcast_in_dim | solution.py:340
  2.5 8.6 %all-to-all-start = ((bf16[8,384,128]{2,1,0:T(8,128)(2,1)}), bf16[8,384,128]{2,1,0:T(8,128)(2,1)S(1)}, u32[]{:S(2)}, u32[]{:S(2)}) async-start(bf16[8,384,128]{2,1,0:T(8,128)(2,1)} %broadcast_in_dim.26), calls=%async_computation | async-start | bytes 1572864 | tf_op jit(solution)/shard_map/all_to_all | solution.py:340
  11.1 0.0 copy-done.10
  11.1 2.4 %collective-permute-start = (bf16[384,128]{1,0:T(8,128)(2,1)S(1)}, bf16[384,128]{1,0:T(8,128)(2,1)S(1)}, u32[]{:S(2)}, u32[]{:S(2)}) collective-permute-start(bf16[384,128]{1,0:T(8,128)(2,1)S(1)} %copy-done.10), channel_id=1, source_target_pairs={{0,16},{16,0},{32,48},{48,32},{64,80},{80,64},{96,112},{112,96},{1... | collective-permute-start | bytes 294920 | tf_op jit(solution)/shard_map/ppermute | solution.py:341
  13.5 4.2 %collective-permute-done = bf16[384,128]{1,0:T(8,128)(2,1)S(1)} collective-permute-done((bf16[384,128]{1,0:T(8,128)(2,1)S(1)}, bf16[384,128]{1,0:T(8,128)(2,1)S(1)}, u32[]{:S(2)}, u32[]{:S(2)}) %collective-permute-start) | collective-permute-done | bytes 98336 | tf_op jit(solution)/shard_map/ppermute | solution.py:341
  17.8 0.0 copy-start.1
  17.8 1.6 %collective-permute-start.1 = (bf16[768,128]{1,0:T(8,128)(2,1)S(1)}, bf16[768,128]{1,0:T(8,128)(2,1)S(1)}, u32[]{:S(2)}, u32[]{:S(2)}) collective-permute-start(bf16[768,128]{1,0:T(8,128)(2,1)S(1)} %constant_dynamic-update-slice_fusion.refs_0_), channel_id=1, source_target_pairs={{0,32},{16,48},{32,64},{48,80},{64,96},{80,112},{96,0},{112,16},{1... | collective-permute-start | bytes 589832 | tf_op jit(solution)/shard_map/ppermute | solution.py:338
  19.3 1.7 %collective-permute-start.2 = (bf16[768,128]{1,0:T(8,128)(2,1)S(1)}, bf16[768,128]{1,0:T(8,128)(2,1)S(1)}, u32[]{:S(2)}, u32[]{:S(2)}) collective-permute-start(bf16[768,128]{1,0:T(8,128)(2,1)S(1)} %constant_dynamic-update-slice_fusion.refs_0_), channel_id=1, source_target_pairs={{0,96},{16,112},{32,0},{48,16},{64,32},{80,48},{96,64},{112,80},{1... | collective-permute-start | bytes 589832 | tf_op jit(solution)/shard_map/ppermute | solution.py:338
  21.1 1.8 %collective-permute-start.3 = (bf16[768,128]{1,0:T(8,128)(2,1)S(1)}, bf16[768,128]{1,0:T(8,128)(2,1)S(1)}, u32[]{:S(2)}, u32[]{:S(2)}) collective-permute-start(bf16[768,128]{1,0:T(8,128)(2,1)S(1)} %constant_dynamic-update-slice_fusion.refs_0_), channel_id=1, source_target_pairs={{0,64},{16,80},{32,96},{48,112},{64,0},{80,16},{96,32},{112,48},{1... | collective-permute-start | bytes 589832 | tf_op jit(solution)/shard_map/ppermute | solution.py:338
  22.9 0.0 collective-permute-start.4
  22.9 3.0 %collective-permute-done.1.refs_1_ = bf16[768,128]{1,0:T(8,128)(2,1)S(1)} collective-permute-done((bf16[768,128]{1,0:T(8,128)(2,1)S(1)}, bf16[768,128]{1,0:T(8,128)(2,1)S(1)}, u32[]{:S(2)}, u32[]{:S(2)}) %collective-permute-start.1) | collective-permute-done | bytes 196640 | tf_op jit(solution)/shard_map/ppermute | solution.py:338
  25.9 0.0 collective-permute-start.5
  25.9 3.0 %collective-permute-done.2.refs_2_ = bf16[768,128]{1,0:T(8,128)(2,1)S(1)} collective-permute-done((bf16[768,128]{1,0:T(8,128)(2,1)S(1)}, bf16[768,128]{1,0:T(8,128)(2,1)S(1)}, u32[]{:S(2)}, u32[]{:S(2)}) %collective-permute-start.2) | collective-permute-done | bytes 196640 | tf_op jit(solution)/shard_map/ppermute | solution.py:338
  28.9 0.0 collective-permute-start.6
  28.9 1.7 %collective-permute-done.3.refs_3_ = bf16[768,128]{1,0:T(8,128)(2,1)S(1)} collective-permute-done((bf16[768,128]{1,0:T(8,128)(2,1)S(1)}, bf16[768,128]{1,0:T(8,128)(2,1)S(1)}, u32[]{:S(2)}, u32[]{:S(2)}) %collective-permute-start.3) | collective-permute-done | bytes 196640 | tf_op jit(solution)/shard_map/ppermute | solution.py:338
  30.6 0.0 collective-permute-start.7
  30.6 0.6 stack.119.place
  31.3 0.0 collective-permute-done.4.refs_4_
  31.3 0.0 collective-permute-done.5.refs_5_
  31.3 0.0 copy-start.6
  31.3 0.0 collective-permute-done.6.refs_6_
  31.3 0.0 copy-start.7
  31.3 0.8 collective-permute-done.7.refs_7_
  32.1 0.0 all-to-all-done
  32.1 0.0 copy-done.1
  32.1 0.6 copy-done.8
  32.7 0.3 copy-done
  33.0 27.9 %match.1 = (f32[8,4,384]{2,1,0:T(4,128)}, f32[2,2,4,384]{3,2,1,0:T(4,128)}, f32[2,2,4,384]{3,2,1,0:T(4,128)}, f32[2,2,4,384]{3,2,1,0:T(4,128)}, f32[2,2,4,384]{3,2,1,0:T(4,128)}) custom-call(s32[40]{0:T(128)} %stack.119.place, bf16[3072,128]{1,0:T(8,128)(2,1)} %bitcast.112, bf16[768,128]{1,0:T(8,128)(2,1)} %copy-done.1, bf16[768,128]{1,0:T(8,128)(2,1)} %copy-done.2, ...), custom_call_target="tpu_custom_call" | custom-call | tf_op jit(solution)/shard_map/match/pallas_call | solution.py:274
  61.0 0.1 collective-permute-start.10
  61.0 0.7 slice_bitcast_fusion.3
  61.8 0.0 copy-start.12
  61.8 7.5 %all-to-all-start.1 = ((f32[8,4,384]{2,1,0:T(4,128)}), f32[8,4,384]{2,1,0:T(4,128)S(1)}, u32[]{:S(2)}, u32[]{:S(2)}) async-start(f32[8,4,384]{2,1,0:T(4,128)} %get-tuple-element.11), calls=%async_computation.1 | async-start | bytes 98304 | tf_op jit(solution)/shard_map/all_to_all | solution.py:349
  69.3 2.8 %collective-permute-start.9 = (f32[2,2,4,384]{3,2,1,0:T(4,128)S(1)}, f32[2,2,4,384]{3,2,1,0:T(4,128)S(1)}, u32[]{:S(2)}, u32[]{:S(2)}) collective-permute-start(f32[2,2,4,384]{3,2,1,0:T(4,128)S(1)} %copy-done.16), channel_id=1, source_target_pairs={{0,96},{16,112},{32,0},{48,16},{64,32},{80,48},{96,64},{112,80},{1... | collective-permute-start | bytes 73736 | tf_op jit(solution)/shard_map/ppermute | solution.py:338
  72.1 0.9 %collective-permute-start.8 = (f32[2,2,4,384]{3,2,0,1:T(4,128)S(1)}, f32[2,2,4,384]{3,2,0,1:T(4,128)S(1)}, u32[]{:S(2)}, u32[]{:S(2)}) collective-permute-start(f32[2,2,4,384]{3,2,0,1:T(4,128)S(1)} %copy.4), channel_id=1, source_target_pairs={{0,32},{16,48},{32,64},{48,80},{64,96},{80,112},{96,0},{112,16},{1... | collective-permute-start | bytes 73736 | tf_op jit(solution)/shard_map/ppermute | solution.py:338
  73.1 0.0 collective-permute-done.10
  73.1 1.7 %collective-permute-done.9 = f32[2,2,4,384]{3,2,1,0:T(4,128)S(1)} collective-permute-done((f32[2,2,4,384]{3,2,1,0:T(4,128)S(1)}, f32[2,2,4,384]{3,2,1,0:T(4,128)S(1)}, u32[]{:S(2)}, u32[]{:S(2)}) %collective-permute-start.9) | collective-permute-done | bytes 24608 | tf_op jit(solution)/shard_map/ppermute | solution.py:338
  74.8 2.4 %collective-permute-done.8 = f32[2,2,4,384]{3,2,0,1:T(4,128)S(1)} collective-permute-done((f32[2,2,4,384]{3,2,0,1:T(4,128)S(1)}, f32[2,2,4,384]{3,2,0,1:T(4,128)S(1)}, u32[]{:S(2)}, u32[]{:S(2)}) %collective-permute-start.8) | collective-permute-done | bytes 24608 | tf_op jit(solution)/shard_map/ppermute | solution.py:338
  77.3 0.1 add_select_fusion
  77.3 0.0 collective-permute-start.12
  77.5 0.7 fusion.2
  78.2 0.0 collective-permute-start.11
  78.2 1.2 %collective-permute-done.11.refs_1_ = f32[4,384]{1,0:T(4,128)S(1)} collective-permute-done((f32[4,384]{1,0:T(4,128)S(1)}, f32[4,384]{1,0:T(4,128)S(1)}, u32[]{:S(2)}, u32[]{:S(2)}) %collective-permute-start.11) | collective-permute-done | bytes 6176 | tf_op jit(solution)/shard_map/ppermute | solution.py:353
  79.4 3.2 %collective-permute-done.12.refs_2_ = f32[2,4,384]{2,1,0:T(4,128)S(1)} collective-permute-done((f32[2,4,384]{2,1,0:T(4,128)S(1)}, f32[2,4,384]{2,1,0:T(4,128)S(1)}, u32[]{:S(2)}, u32[]{:S(2)}) %collective-permute-start.12) | collective-permute-done | bytes 12320 | tf_op jit(solution)/shard_map/ppermute | solution.py:351
  82.6 0.0 all-to-all-done.1.one
  82.6 0.1 collective-permute-start.13
  82.7 1.2 %collective-permute-done.13.refs_3_ = f32[2,4,384]{2,1,0:T(4,128)S(1)} collective-permute-done((f32[2,4,384]{2,1,0:T(4,128)S(1)}, f32[2,4,384]{2,1,0:T(4,128)S(1)}, u32[]{:S(2)}, u32[]{:S(2)}) %collective-permute-start.13) | collective-permute-done | bytes 12320 | tf_op jit(solution)/shard_map/ppermute | solution.py:355
  83.9 0.6 copy-done.14
  84.4 1.6 %flow.1 = (f32[2,384]{1,0:T(2,128)}, f32[2,384]{1,0:T(2,128)}) custom-call(s32[40]{0:T(128)} %stack.119.place, f32[8,4,384]{2,1,0:T(4,128)} %copy-done.9, f32[4,384]{1,0:T(4,128)} %get-tuple-element.17.refs_0_, f32[4,384]{1,0:T(4,128)} %copy-done.15, f32[2,4,384]{2,1,0:T(4,128)} %copy-done.13, f32[2,4,384]{2,1,0:T(4,128)} %copy-done.14), custom_call_target="tpu_custom_call" | custom-call | tf_op jit(solution)/shard_map/flow/pallas_call | solution.py:321
  (44 shorter events, 0.3 us)
Async XLA Ops:
  2.5 8.6 %copy-start.10 = (bf16[384,128]{1,0:T(8,128)(2,1)S(1)}, bf16[384,128]{1,0:T(8,128)(2,1)}, u32[]{:S(2)}) copy-start(bf16[384,128]{1,0:T(8,128)(2,1)} %param.3) | copy-start | bytes 294916
  2.5 29.6 %all-to-all-start = ((bf16[8,384,128]{2,1,0:T(8,128)(2,1)}), bf16[8,384,128]{2,1,0:T(8,128)(2,1)S(1)}, u32[]{:S(2)}, u32[]{:S(2)}) async-start(bf16[8,384,128]{2,1,0:T(8,128)(2,1)} %broadcast_in_dim.26), calls=%async_computation | async-start | bytes 1572864 | tf_op jit(solution)/shard_map/all_to_all | solution.py:340
  11.1 6.6 %collective-permute-start = (bf16[384,128]{1,0:T(8,128)(2,1)S(1)}, bf16[384,128]{1,0:T(8,128)(2,1)S(1)}, u32[]{:S(2)}, u32[]{:S(2)}) collective-permute-start(bf16[384,128]{1,0:T(8,128)(2,1)S(1)} %copy-done.10), channel_id=1, source_target_pairs={{0,16},{16,0},{32,48},{48,32},{64,80},{80,64},{96,112},{112,96},{1... | collective-permute-start | bytes 294920 | tf_op jit(solution)/shard_map/ppermute | solution.py:341
  17.8 14.3 %copy-start.1 = (bf16[768,128]{1,0:T(8,128)(2,1)}, bf16[768,128]{1,0:T(8,128)(2,1)S(1)}, u32[]{:S(2)}) copy-start(bf16[768,128]{1,0:T(8,128)(2,1)S(1)} %constant_dynamic-update-slice_fusion.refs_0_) | copy-start | bytes 589828
  17.8 8.1 %collective-permute-start.1 = (bf16[768,128]{1,0:T(8,128)(2,1)S(1)}, bf16[768,128]{1,0:T(8,128)(2,1)S(1)}, u32[]{:S(2)}, u32[]{:S(2)}) collective-permute-start(bf16[768,128]{1,0:T(8,128)(2,1)S(1)} %constant_dynamic-update-slice_fusion.refs_0_), channel_id=1, source_target_pairs={{0,32},{16,48},{32,64},{48,80},{64,96},{80,112},{96,0},{112,16},{1... | collective-permute-start | bytes 589832 | tf_op jit(solution)/shard_map/ppermute | solution.py:338
  19.3 9.6 %collective-permute-start.2 = (bf16[768,128]{1,0:T(8,128)(2,1)S(1)}, bf16[768,128]{1,0:T(8,128)(2,1)S(1)}, u32[]{:S(2)}, u32[]{:S(2)}) collective-permute-start(bf16[768,128]{1,0:T(8,128)(2,1)S(1)} %constant_dynamic-update-slice_fusion.refs_0_), channel_id=1, source_target_pairs={{0,96},{16,112},{32,0},{48,16},{64,32},{80,48},{96,64},{112,80},{1... | collective-permute-start | bytes 589832 | tf_op jit(solution)/shard_map/ppermute | solution.py:338
  21.1 9.5 %collective-permute-start.3 = (bf16[768,128]{1,0:T(8,128)(2,1)S(1)}, bf16[768,128]{1,0:T(8,128)(2,1)S(1)}, u32[]{:S(2)}, u32[]{:S(2)}) collective-permute-start(bf16[768,128]{1,0:T(8,128)(2,1)S(1)} %constant_dynamic-update-slice_fusion.refs_0_), channel_id=1, source_target_pairs={{0,64},{16,80},{32,96},{48,112},{64,0},{80,16},{96,32},{112,48},{1... | collective-permute-start | bytes 589832 | tf_op jit(solution)/shard_map/ppermute | solution.py:338
  22.9 8.4 %collective-permute-start.4 = (bf16[768,128]{1,0:T(8,128)(2,1)S(1)}, bf16[768,128]{1,0:T(8,128)(2,1)S(1)}, u32[]{:S(2)}, u32[]{:S(2)}) collective-permute-start(bf16[768,128]{1,0:T(8,128)(2,1)S(1)} %constant_dynamic-update-slice_fusion.refs_0_), channel_id=1, source_target_pairs={{0,1},{1,0},{2,3},{3,2},{4,5},{5,4},{6,7},{7,6},{8,9},{9,8},{10,11... | collective-permute-start | bytes 589832 | tf_op jit(solution)/shard_map/ppermute | solution.py:343
  25.9 6.2 %copy-start.2 = (bf16[768,128]{1,0:T(8,128)(2,1)}, bf16[768,128]{1,0:T(8,128)(2,1)S(1)}, u32[]{:S(2)}) copy-start(bf16[768,128]{1,0:T(8,128)(2,1)S(1)} %collective-permute-done.1.refs_1_) | copy-start | bytes 589828
  25.9 5.4 %collective-permute-start.5 = (bf16[768,128]{1,0:T(8,128)(2,1)S(1)}, bf16[768,128]{1,0:T(8,128)(2,1)S(1)}, u32[]{:S(2)}, u32[]{:S(2)}) collective-permute-start(bf16[768,128]{1,0:T(8,128)(2,1)S(1)} %collective-permute-done.1.refs_1_), channel_id=1, source_target_pairs={{0,1},{1,0},{2,3},{3,2},{4,5},{5,4},{6,7},{7,6},{8,9},{9,8},{10,11... | collective-permute-start | bytes 589832 | tf_op jit(solution)/shard_map/ppermute | solution.py:343
  28.9 3.2 %copy-start.3 = (bf16[768,128]{1,0:T(8,128)(2,1)}, bf16[768,128]{1,0:T(8,128)(2,1)S(1)}, u32[]{:S(2)}) copy-start(bf16[768,128]{1,0:T(8,128)(2,1)S(1)} %collective-permute-done.2.refs_2_) | copy-start | bytes 589828
  28.9 2.4 %collective-permute-start.6 = (bf16[768,128]{1,0:T(8,128)(2,1)S(1)}, bf16[768,128]{1,0:T(8,128)(2,1)S(1)}, u32[]{:S(2)}, u32[]{:S(2)}) collective-permute-start(bf16[768,128]{1,0:T(8,128)(2,1)S(1)} %collective-permute-done.2.refs_2_), channel_id=1, source_target_pairs={{0,1},{1,0},{2,3},{3,2},{4,5},{5,4},{6,7},{7,6},{8,9},{9,8},{10,11... | collective-permute-start | bytes 589832 | tf_op jit(solution)/shard_map/ppermute | solution.py:343
  30.6 1.5 %copy-start.4 = (bf16[768,128]{1,0:T(8,128)(2,1)}, bf16[768,128]{1,0:T(8,128)(2,1)S(1)}, u32[]{:S(2)}) copy-start(bf16[768,128]{1,0:T(8,128)(2,1)S(1)} %collective-permute-done.3.refs_3_) | copy-start | bytes 589828
  30.6 1.4 %collective-permute-start.7 = (bf16[768,128]{1,0:T(8,128)(2,1)S(1)}, bf16[768,128]{1,0:T(8,128)(2,1)S(1)}, u32[]{:S(2)}, u32[]{:S(2)}) collective-permute-start(bf16[768,128]{1,0:T(8,128)(2,1)S(1)} %collective-permute-done.3.refs_3_), channel_id=1, source_target_pairs={{0,1},{1,0},{2,3},{3,2},{4,5},{5,4},{6,7},{7,6},{8,9},{9,8},{10,11... | collective-permute-start | bytes 589832 | tf_op jit(solution)/shard_map/ppermute | solution.py:343
  31.3 0.8 copy-start.5
  31.3 0.8 copy-start.6
  31.3 0.8 copy-start.7
  32.1 0.7 copy-start.8
  32.1 1.0 %copy-start = (bf16[8,384,128]{2,1,0:T(8,128)(2,1)}, bf16[8,384,128]{2,1,0:T(8,128)(2,1)S(1)}, u32[]{:S(2)}) copy-start(bf16[8,384,128]{2,1,0:T(8,128)(2,1)S(1)} %all-to-all-done) | copy-start | bytes 2359300
  60.9 0.8 copy-start.11
  61.0 12.1 %collective-permute-start.10 = (f32[2,2,4,384]{3,2,1,0:T(4,128)}, f32[2,2,4,384]{3,2,1,0:T(4,128)S(1)}, u32[]{:S(2)}, u32[]{:S(2)}) collective-permute-start(f32[2,2,4,384]{3,2,1,0:T(4,128)} %get-tuple-element.15), channel_id=1, source_target_pairs={{0,64},{16,80},{32,96},{48,112},{64,0},{80,16},{96,32},{112,48},{1... | collective-permute-start | bytes 73736 | tf_op jit(solution)/shard_map/ppermute | solution.py:338
  61.8 7.6 %copy-start.16 = (f32[2,2,4,384]{3,2,1,0:T(4,128)S(1)}, f32[2,2,4,384]{3,2,1,0:T(4,128)}, u32[]{:S(2)}) copy-start(f32[2,2,4,384]{3,2,1,0:T(4,128)} %get-tuple-element.14) | copy-start | bytes 73732
  61.8 10.3 %copy-start.12 = (f32[2,2,4,384]{3,2,1,0:T(4,128)S(1)}, f32[2,2,4,384]{3,2,1,0:T(4,128)}, u32[]{:S(2)}) copy-start(f32[2,2,4,384]{3,2,1,0:T(4,128)} %get-tuple-element.13) | copy-start | bytes 73732
  61.8 20.8 %all-to-all-start.1 = ((f32[8,4,384]{2,1,0:T(4,128)}), f32[8,4,384]{2,1,0:T(4,128)S(1)}, u32[]{:S(2)}, u32[]{:S(2)}) async-start(f32[8,4,384]{2,1,0:T(4,128)} %get-tuple-element.11), calls=%async_computation.1 | async-start | bytes 98304 | tf_op jit(solution)/shard_map/all_to_all | solution.py:349
  69.3 5.4 %collective-permute-start.9 = (f32[2,2,4,384]{3,2,1,0:T(4,128)S(1)}, f32[2,2,4,384]{3,2,1,0:T(4,128)S(1)}, u32[]{:S(2)}, u32[]{:S(2)}) collective-permute-start(f32[2,2,4,384]{3,2,1,0:T(4,128)S(1)} %copy-done.16), channel_id=1, source_target_pairs={{0,96},{16,112},{32,0},{48,16},{64,32},{80,48},{96,64},{112,80},{1... | collective-permute-start | bytes 73736 | tf_op jit(solution)/shard_map/ppermute | solution.py:338
  72.1 5.0 %collective-permute-start.8 = (f32[2,2,4,384]{3,2,0,1:T(4,128)S(1)}, f32[2,2,4,384]{3,2,0,1:T(4,128)S(1)}, u32[]{:S(2)}, u32[]{:S(2)}) collective-permute-start(f32[2,2,4,384]{3,2,0,1:T(4,128)S(1)} %copy.4), channel_id=1, source_target_pairs={{0,32},{16,48},{32,64},{48,80},{64,96},{80,112},{96,0},{112,16},{1... | collective-permute-start | bytes 73736 | tf_op jit(solution)/shard_map/ppermute | solution.py:338
  77.3 5.2 %collective-permute-start.12 = (f32[2,4,384]{2,1,0:T(4,128)S(1)}, f32[2,4,384]{2,1,0:T(4,128)S(1)}, u32[]{:S(2)}, u32[]{:S(2)}) collective-permute-start(f32[2,4,384]{2,1,0:T(4,128)S(1)} %add_select_fusion), channel_id=1, source_target_pairs={{0,16},{16,0},{32,48},{48,32},{64,80},{80,64},{96,112},{112,96},{1... | collective-permute-start | bytes 36872 | tf_op jit(solution)/shard_map/ppermute | solution.py:351
  78.2 1.2 %collective-permute-start.11 = (f32[4,384]{1,0:T(4,128)S(1)}, f32[4,384]{1,0:T(4,128)S(1)}, u32[]{:S(2)}, u32[]{:S(2)}) collective-permute-start(f32[4,384]{1,0:T(4,128)S(1)} %get-tuple-element.34), channel_id=1, source_target_pairs={{0,1},{1,0},{2,3},{3,2},{4,5},{5,4},{6,7},{7,6},{8,9},{9,8},{10,11... | collective-permute-start | bytes 18440 | tf_op jit(solution)/shard_map/ppermute | solution.py:353
  79.3 4.5 %copy-start.15 = (f32[4,384]{1,0:T(4,128)}, f32[4,384]{1,0:T(4,128)S(1)}, u32[]{:S(2)}) copy-start(f32[4,384]{1,0:T(4,128)S(1)} %collective-permute-done.11.refs_1_) | copy-start | bytes 18436
  82.6 1.3 %copy-start.13 = (f32[2,4,384]{2,1,0:T(4,128)}, f32[2,4,384]{2,1,0:T(4,128)S(1)}, u32[]{:S(2)}) copy-start(f32[2,4,384]{2,1,0:T(4,128)S(1)} %collective-permute-done.12.refs_2_) | copy-start | bytes 36868
  82.6 1.3 %copy-start.9 = (f32[8,4,384]{2,1,0:T(4,128)}, f32[8,4,384]{2,1,0:T(4,128)S(1)}, u32[]{:S(2)}) copy-start(f32[8,4,384]{2,1,0:T(4,128)S(1)} %all-to-all-done.1.one) | copy-start | bytes 147460
  82.6 1.3 %collective-permute-start.13 = (f32[2,4,384]{2,1,0:T(4,128)S(1)}, f32[2,4,384]{2,1,0:T(4,128)S(1)}, u32[]{:S(2)}, u32[]{:S(2)}) collective-permute-start(f32[2,4,384]{2,1,0:T(4,128)S(1)} %collective-permute-done.12.refs_2_), channel_id=1, source_target_pairs={{0,1},{1,0},{2,3},{3,2},{4,5},{5,4},{6,7},{7,6},{8,9},{9,8},{10,11... | collective-permute-start | bytes 36872 | tf_op jit(solution)/shard_map/ppermute | solution.py:355
  83.8 0.6 copy-start.14
